TPU v7x, 256 devices: a whole 4x4x8 slice. The times are simulated.
256 devices in a mesh: dom: 64 (over y, z, core), feat: 4 (over x).
Axes of the slice: x: 4, y: 4, z: 8, core: 2. Of those that a mesh axis runs over, the one named last changes fastest.
Arguments:
- features: bfloat16 [16384, 512], P('dom', 'feat'), may hold values from -6 to 6
- hub_feats: bfloat16 [2048, 256], P('dom'), may hold values from -6 to 6
- nbr_owner: int32 [8, 32768, 1], P(None, 'dom'), may hold values from 0 to 63; in each aligned block of 512 rows (0 to 511, 512 to 1023, ..., all dimensions but the last counted through in order) at most 16 rows name the same one
- nbr_row: int32 [8, 32768], P(None, 'dom'), may hold values from 0 to 511
- hub_ids: int32 [32768, 4], P('dom'), may hold values from 0 to 2047
- w_self: bfloat16 [256, 256], replicated, may hold values from -0.375 to 0.375
- w_nbr: bfloat16 [256, 256], replicated, may hold values from -0.375 to 0.375
- grad_out: bfloat16 [16384, 512], P('dom', 'feat'), may hold values from -6 to 6
Outputs:
- outputs: bfloat16 [16384, 512], P('dom', 'feat')
- grad_features: bfloat16 [16384, 512], P('dom', 'feat')
- grad_hubs: float32 [2048, 256], P('dom', 'feat')
- grad_self: float32 [256, 256], P('feat')
- grad_nbr: float32 [256, 256], P('feat')
Inputs may be any that keep to these rules, and one draw needn't show every extreme that they name: `nbr_owner`: for each sample index k, among the 512 targets of one partition at most 16 have their k-th neighbour on one owner; that many is reached.
All inputs are finite; a program needn't handle non-finite values.
Results may differ from a plain program's by a relative error of at most 0.0054.
Values may be sent and summed in bfloat16 or wider, within the bound.
No kernel may reach another device: no remote copies, remote signals or barrier semaphores. Data moves between devices by JAX's collectives and lax.ppermute only.
A program may use at most 64 MiB of HBM per device.

v0:
```python
import functools

import jax
import jax.numpy as jnp
from jax import lax
from jax.experimental import pallas as pl
from jax.experimental.pallas import tpu as pltpu
from jax.sharding import Mesh, PartitionSpec as P

NY, NZ, NC, NX = 4, 8, 2, 4
V = 512
HALF = 256
COLS = 128
HUB_ROWS = 16
BLOCK = HALF + HUB_ROWS
ROWS = (NZ + 1) * HALF
PARTS = NC * NY
WROWS = 256
DISTINCT = 4
BF = jnp.bfloat16
F32 = jnp.float32
VM = pl.BlockSpec(memory_space=pltpu.VMEM)
PLAIN = (((1,), (0,)), ((), ()))
LAST = (((1,), (1,)), ((), ()))
FIRST = (((0,), (0,)), ((), ()))


def dot(a, b, dims=PLAIN, **kw):
    return lax.dot_general(a, b, dims, preferred_element_type=F32, **kw)


def shift(x, axis, size, step):
    return lax.ppermute(x, axis, [(i, (i + step) % size) for i in range(size)])


def swap(x, axis, size, mask):
    return lax.ppermute(x, axis, [(i, i ^ mask) for i in range(size)])


MASKS = (0, 2, 1, 3)


def three(x, axis, size, each=False):
    own = x[0] if each else x
    return [own] + [swap(x[mask] if each else x, axis, size, mask) for mask in MASKS[1:]]


def call(kernel, outs, inputs, name, scratch=(), flops=0, mib=16, far=0):
    return pl.pallas_call(
        kernel,
        out_shape=outs,
        in_specs=[VM] * (len(inputs) - far) + [pl.BlockSpec(memory_space=pl.ANY)] * far,
        out_specs=jax.tree.map(lambda _: VM, outs),
        scratch_shapes=list(scratch),
        compiler_params=pltpu.CompilerParams(vmem_limit_bytes=mib << 20),
        cost_estimate=pl.CostEstimate(flops=flops, bytes_accessed=1 << 18, transcendentals=0),
        name=name,
    )(*inputs)


def shaped(shape, dtype):
    return jax.ShapeDtypeStruct(shape, dtype)


def prepare_kernel(
    feat, cot, hub, owner, row, hub_id, ids_ref, mine_ref, both,
    owner_scr, row_scr, hub_id_scr, hub_scr, sems,
):
    parity, half = lax.axis_index("x") // 2, lax.axis_index("x") % 2
    pairs = (
        (owner, owner_scr),
        (row, row_scr),
        (hub_id, hub_id_scr),
        (hub, hub_scr),
        (feat, mine_ref.at[pl.ds(0, HALF)]),
        (feat, both.at[pl.ds(0, HALF)]),
        (cot, both.at[pl.ds(HALF, HALF)]),
    )
    copies = [pltpu.make_async_copy(a, b, sems.at[i]) for i, (a, b) in enumerate(pairs)]
    for copy in copies:
        copy.start()
    for copy in copies:
        copy.wait()
    ids_ref[0:8] = owner_scr[...].reshape(8, V) * V + row_scr[...]
    ids_ref[8:12] = hub_id_scr[...]
    ids_ref[12:16] = jnp.full((4, V), -1, jnp.int32)
    pick = lax.broadcasted_iota(jnp.int32, (HUB_ROWS, 2 * HUB_ROWS), 1) == (
        2 * lax.broadcasted_iota(jnp.int32, (HUB_ROWS, 2 * HUB_ROWS), 0) + parity
    )
    columns = hub_scr[:, pl.ds(pl.multiple_of(half * COLS, COLS), COLS)]
    mine_ref[HALF:BLOCK] = dot(pick.astype(F32).astype(BF), columns).astype(BF)


def counts_kernel(ids0, ids1, ids2, ids3, out_ref, ids_scr, key_scr):
    y, z, c, x = (lax.axis_index(a) for a in ("y", "z", "c", "x"))
    parity = x // 2
    rows = lax.broadcasted_iota(jnp.int32, (16, 16, 128), 0) * 16 + lax.broadcasted_iota(
        jnp.int32, (16, 16, 128), 1
    )
    rows = rows.astype(F32).astype(BF)
    level = lax.broadcasted_iota(jnp.int32, (8, V), 0)
    column = y * (NZ * NC) + c
    mask = (NY - 1) * (NZ * NC) + (NC - 1)

    def allmax(a):
        for s in (4, 2, 1):
            a = jnp.maximum(a, pltpu.roll(a, s, 0))
        return a

    def allsum(a):
        for s in (4, 2, 1):
            a = a + pltpu.roll(a, s, 0)
        return a

    def extract(keys):
        top = allmax(keys)
        hit = keys == top
        return jnp.where(hit, -1.0, keys), top, allsum(jnp.where(hit, 1.0, 0.0))

    def pair(a):
        return jnp.concatenate([a, a], 0).astype(BF)

    for dy, ids_ref in zip(MASKS, (ids0, ids1, ids2, ids3)):
        for dc in range(NC):
            ids_scr[dc * NY + dy] = ids_ref[dc]

    def part(index, carry):
        ids = ids_scr[index]
        flat, hub = ids[0:8], ids[8:16]
        here = ((flat >> 9) & mask) == column
        here = here & ((flat & 1) == parity)
        keys = jnp.where(here, (((flat >> 10) - z) & 7) * HALF + ((flat >> 1) & 255), -1).astype(F32)
        here = (((hub >> 5) & mask) == column) & (level < 4)
        hub_row = (((hub >> 6) - z) & 7) * 32 + ((hub & 1) ^ parity) * 16 + ((hub >> 1) & 15)
        hub_keys = jnp.where(here, hub_row, -1).astype(F32)
        found, hub_found = [], []
        for _ in range(DISTINCT):
            keys, top, times = extract(keys)
            found.append((top, pair(times)))
        for _ in range(4):
            hub_keys, top, times = extract(hub_keys)
            hub_found.append((pair(top), pair(times)))
        for tile in range(V // 128):
            lanes = slice(tile * 128, (tile + 1) * 128)
            for delta in range(NZ):
                block = jnp.zeros((16, 16, 128), BF)
                for top, times in found:
                    match = pair(top[:, lanes] - float(HALF * delta))[None] == rows
                    block = jnp.where(match, times[:, lanes][None], block)
                out_ref[index, delta * HALF : (delta + 1) * HALF, lanes] = block.reshape(HALF, 128)
            block = jnp.zeros((16, 16, 128), BF)
            for top, times in hub_found:
                block = jnp.where(top[:, lanes][None] == rows, times[:, lanes][None], block)
            out_ref[index, NZ * HALF : ROWS, lanes] = block.reshape(HALF, 128)

        def more(keys):
            keys, top, times = extract(keys)
            key_scr[0] = top
            key_scr[1] = times

            def fix(step, inner):
                delta = step % NZ
                lanes = pl.ds(pl.multiple_of(step // NZ * 128, 128), 128)
                span = pl.ds(pl.multiple_of(delta * HALF, HALF), HALF)
                wanted = key_scr[0, :, lanes] - (delta * HALF).astype(F32)
                block = out_ref[index, span, lanes].reshape(16, 16, 128)
                block = jnp.where(pair(wanted)[None] == rows, pair(key_scr[1, :, lanes])[None], block)
                out_ref[index, span, lanes] = block.reshape(HALF, 128)
                return inner

            lax.fori_loop(0, NZ * (V // 128), fix, 0)
            return keys

        lax.while_loop(lambda keys: jnp.max(keys) >= 0, more, keys)
        return carry

    lax.fori_loop(0, PARTS, part, 0)


def far_sums_kernel(counts, t0, t1, t2, t7, t34, t65, sums_ref, turned_ref, table):
    blocks = {0: t0[...], 1: t1[...], 2: t2[...], 7: t7[...]}
    blocks[3], blocks[4] = t34[0:BLOCK], t34[BLOCK : 2 * BLOCK]
    blocks[6], blocks[5] = t65[0:BLOCK], t65[BLOCK : 2 * BLOCK]
    for delta in range(NZ):
        table[delta * HALF : (delta + 1) * HALF] = blocks[delta][0:HALF]
        start = NZ * HALF + delta * 2 * HUB_ROWS
        table[start : start + HUB_ROWS] = blocks[delta][HALF:BLOCK]
        table[start + HUB_ROWS : start + 2 * HUB_ROWS] = jnp.zeros((HUB_ROWS, COLS), BF)
    turned_ref[...] = table[...].T

    for dy in range(NY):
        sums_ref[dy] = dot(turned_ref[...], counts[NY + dy]).astype(BF)


def near_sums_kernel(counts, turned, sums_ref):
    for dy in range(NY):
        sums_ref[dy] = dot(turned[...], counts[dy])


def arrange_kernel(fg0, fg1, fg23, ws_ref, turned_ref, cot_ref, pre_ref, order_ref, back_ref, scr):
    x = lax.axis_index("x")
    for mask, (ref, start) in enumerate(((fg0, 0), (fg1, 0), (fg23, 0), (fg23, V))):
        scr[x ^ mask] = ref[start : start + V]
    rows = []
    for start in (0, HALF):
        quarters = [scr[q, start : start + HALF] for q in range(NX)]
        rows.append(
            jnp.concatenate(
                [jnp.concatenate(quarters[0:2], 1), jnp.concatenate(quarters[2:4], 1)], 0
            )
        )
    turned_ref[...] = rows[0].T
    cot_ref[...] = rows[1]
    pre_ref[...] = dot(rows[0], ws_ref[...])
    first = lax.broadcasted_iota(jnp.int32, (V, V), 0)
    second = lax.broadcasted_iota(jnp.int32, (V, V), 1)
    order_ref[...] = ((first % HALF) * 2 + first // HALF == second).astype(F32).astype(BF)
    back_ref[...] = ((second % HALF) * 2 + second // HALF == first).astype(F32).astype(BF)


def dense_kernel(
    turned_ref, cot_ref, pre_ref, order_ref, back_ref, s0, s1, s2, s3, ws_ref, wn_ref,
    out_ref, message_ref, self_ref,
    s_scr, o_scr, w_scr,
):
    x = lax.axis_index("x")
    parity, half = x // 2, x % 2
    for mask, ref in zip(MASKS, (s0, s1, s2, s3)):
        s_scr[x ^ mask] = ref[...]
    mean_t = jnp.concatenate(
        [
            s_scr[0].astype(F32) + s_scr[2].astype(F32),
            s_scr[1].astype(F32) + s_scr[3].astype(F32),
        ],
        0,
    )
    mean_t = (mean_t / 12.0).astype(BF)
    mean = dot(order_ref[...], mean_t, LAST).astype(BF)
    pre = pre_ref[...] + dot(mean, wn_ref[...])
    sig = jax.nn.sigmoid(pre)
    value = (pre * sig).astype(BF)
    grad_pre = (cot_ref[...].astype(F32) * sig * (1.0 + pre * (1.0 - sig))).astype(BF)
    for q in range(2):
        for h in range(2):
            o_scr[q * 2 + h] = value[q * HALF : (q + 1) * HALF, h * COLS : (h + 1) * COLS]
    out_ref[...] = o_scr[x]
    rows = pl.ds(pl.multiple_of(half * COLS, COLS), COLS)
    natural = dot(back_ref[...], grad_pre).astype(BF)
    message_ref[0:V] = (dot(natural, wn_ref[rows, :], LAST) / 12.0).astype(BF)
    own_self = dot(grad_pre, ws_ref[rows, :], LAST)
    self_ref[...] = jnp.where(parity == 0, own_self[0:HALF], own_self[HALF:V])
    w_scr[0] = dot(turned_ref[...], grad_pre)
    w_scr[1] = dot(mean_t, natural)
    quarter = pl.ds(pl.multiple_of(x * 64, 64), 64)
    for which in range(2):
        part = w_scr[which, quarter, :]
        for h in range(2):
            start = V + which * 128 + h * 64
            message_ref[start : start + 64, :] = part[:, h * COLS : (h + 1) * COLS].astype(BF)


def block_sum(counts, base, messages, block, total=None):
    span = slice(block * HALF, (block + 1) * HALF)
    for index, ref in enumerate(messages):
        dy = base + index // NY * NY + MASKS[index % NY]
        term = dot(counts[dy, span], ref[0:V])
        total = term if total is None else total + term
    return total


FIRST_BLOCKS = (4, 5, NZ)


def near_grads_kernel(counts, m0, m1, m2, m3, out_ref):
    for index, block in enumerate(FIRST_BLOCKS):
        out_ref[index] = block_sum(counts, 0, (m0, m1, m2, m3), block)


def first_grads_kernel(
    counts, m0, m1, m2, m3, o0, o1, o2, o3, near, up_ref, down_ref, hub_ref, skip_ref
):
    parity = lax.axis_index("x") // 2
    others = (o0, o1, o2, o3)
    blocks = [block_sum(counts, NY, others, block, near[index]) for index, block in enumerate(FIRST_BLOCKS)]
    hubs = blocks[2]
    lane = lax.broadcasted_iota(jnp.int32, (HUB_ROWS, COLS), 1)
    low = (lane < 64) == (parity == 0)
    for delta in range(NZ):
        start = delta * 2 * HUB_ROWS
        mine = hubs[start : start + HUB_ROWS]
        rest = pltpu.roll(hubs[start + HUB_ROWS : start + 2 * HUB_ROWS], 64, 1)
        hub_ref[delta] = jnp.where(low, mine, rest)
    tail = slice(V, V + WROWS)
    sums = [
        (a[tail].astype(F32) + b[tail].astype(F32)) + (c[tail].astype(F32) + d[tail].astype(F32))
        for a, b, c, d in ((m0, m1, m2, m3), others)
    ]
    weight = (sums[0] + sums[1]).astype(BF)
    skip_ref[...] = hub_ref[4]
    for index, (hub_delta, ref) in enumerate(((3, up_ref), (5, down_ref))):
        ref[0:HALF] = blocks[index].astype(BF)
        ref[HALF:BLOCK] = hub_ref[hub_delta].astype(BF)
        ref[BLOCK:] = weight


def rest_grads_kernel(counts, m0, m1, m2, m3, o0, o1, o2, o3, out_ref, *, blocks):
    for index, block in enumerate(blocks):
        out_ref[index] = block_sum(counts, 0, (m0, m1, m2, m3, o0, o1, o2, o3), block)


def hop_kernel(got, rest, hubs, skip, turn, next_ref, token_ref, *, index, hub_delta):
    next_ref[0:HALF] = (got[0:HALF].astype(F32) + rest[index]).astype(BF)
    hub = got[HALF:BLOCK].astype(F32) + hubs[hub_delta]
    if hub_delta == 2:
        hub = hub + skip[...]
    next_ref[HALF:BLOCK] = hub.astype(BF)
    next_ref[BLOCK:] = got[BLOCK:]
    token_ref[...] = jnp.zeros_like(token_ref)


def last_hop_kernel(up, rest, turn, next_up, token_ref):
    next_up[0:HALF] = (up[0:HALF].astype(F32) + rest[0]).astype(BF)
    next_up[HALF:] = up[BLOCK:]
    token_ref[...] = jnp.zeros_like(token_ref)


def hub_kernel(up, down, hubs, turn, hub_sum):
    hub_sum[...] = up[HALF:BLOCK].astype(F32) + down[HALF:BLOCK].astype(F32) + hubs[0]


def final_kernel(
    self_ref, rest, first, up1, up2, up3, up4, down1, down2, down3, hub_sum,
    feat_ref, hub_ref, gself_ref, gnbr_ref, w_scr,
):
    z = lax.axis_index("z")
    total = rest[1] + up4[0:HALF].astype(F32) + down3[0:HALF].astype(F32)
    feat_ref[...] = (self_ref[...] + total).astype(BF)
    hubs = hub_sum[...]
    shape = (2 * HUB_ROWS, HUB_ROWS)
    target = lax.broadcasted_iota(jnp.int32, shape, 0)
    source = lax.broadcasted_iota(jnp.int32, shape, 1)
    spread = [
        dot((target == 2 * source + q).astype(F32), hubs[:, q * 64 : (q + 1) * 64], precision=lax.Precision.HIGHEST)
        for q in range(2)
    ]
    hub_ref[...] = spread[0] + spread[1]
    arrived = {0: first, 7: up1, 6: up2, 5: up3, 1: down1, 2: down2, 3: down3}
    for step in range(NZ):
        if step == 4:
            w_scr[(z + step) % NZ] = up4[HALF:]
        else:
            w_scr[(z + step) % NZ] = arrived[step][BLOCK:]
    weight = w_scr[0].astype(F32)
    for step in range(1, NZ):
        weight = weight + w_scr[step].astype(F32)
    gself_ref[...] = jnp.concatenate([weight[0:64], weight[64:128]], 1)
    gnbr_ref[...] = jnp.concatenate([weight[128:192], weight[192:256]], 1)


def body(features, hub_feats, nbr_owner, nbr_row, hub_ids, w_self, w_nbr, grad_out):
    ids, mine, fg = call(
        prepare_kernel,
        (pltpu.VMEM((16, V), jnp.int32), pltpu.VMEM((BLOCK, COLS), BF), pltpu.VMEM((V, COLS), BF)),
        (features, grad_out, hub_feats, nbr_owner.reshape(8, 1, V), nbr_row, hub_ids.T),
        "prepare",
        scratch=[
            pltpu.VMEM((8, 1, V), jnp.int32),
            pltpu.VMEM((8, V), jnp.int32),
            pltpu.VMEM((4, V), jnp.int32),
            pltpu.VMEM((2 * HUB_ROWS, 256), BF),
            pltpu.SemaphoreType.DMA((7,)),
        ],
        far=6,
        mib=56,
    )

    fg1 = swap(fg, "x", NX, 1)
    fg23 = swap(jnp.concatenate([fg, fg1], 0), "x", NX, 2)

    pair = jnp.stack([ids, swap(ids, "c", NC, 1)])
    t1, t7, t2 = shift(mine, "z", NZ, -1), shift(mine, "z", NZ, 1), shift(mine, "z", NZ, -2)
    pairs = three(pair, "y", NY)
    t34 = shift(jnp.concatenate([t1, t2], 0), "z", NZ, -2)
    t65 = shift(jnp.concatenate([mine, t7], 0), "z", NZ, 2)
    counts = call(
        counts_kernel,
        pltpu.VMEM((PARTS, ROWS, V), BF),
        (*pairs,),
        "counts",
        flops=1 << 34,
        scratch=[pltpu.VMEM((PARTS, 16, V), jnp.int32), pltpu.VMEM((2, 8, V), F32)],
        mib=8,
    )

    far, turned = call(
        far_sums_kernel,
        (shaped((NY, COLS, V), BF), shaped((COLS, ROWS), BF)),
        (counts, mine, t1, t2, t7, t34, t65),
        "far_sums",
        scratch=[pltpu.VMEM((ROWS, COLS), BF)],
        flops=1 << 31,
    )
    got = swap(far, "c", NC, 1)
    near = call(
        near_sums_kernel, shaped((NY, COLS, V), F32), (counts, turned), "near_sums", flops=1 << 31
    )
    both = near + got.astype(F32)
    parts = three(both.astype(BF), "y", NY, each=True)
    total = both[0] + parts[1].astype(F32) + parts[2].astype(F32) + parts[3].astype(F32)
    sums = three(total.astype(BF), "x", NX)

    arranged = call(
        arrange_kernel,
        (
            shaped((256, V), BF),
            shaped((V, 256), BF),
            shaped((V, 256), F32),
            shaped((V, V), BF),
            shaped((V, V), BF),
        ),
        (fg, fg1, fg23, w_self),
        "arrange",
        scratch=[pltpu.VMEM((NX, V, COLS), BF)],
        flops=1 << 28,
    )
    outputs, message, self_term = call(
        dense_kernel,
        (shaped((HALF, COLS), BF), shaped((V + WROWS, COLS), BF), shaped((HALF, COLS), F32)),
        (*arranged, *sums, w_self, w_nbr),
        "dense",
        scratch=[
            pltpu.VMEM((4, COLS, V), BF),
            pltpu.VMEM((4, HALF, COLS), BF),
            pltpu.VMEM((2, 256, 256), F32),
        ],
        flops=1 << 30,
    )

    messages = three(message, "y", NY)
    others = [swap(m, "c", NC, 1) for m in messages]
    near_grads = call(
        near_grads_kernel,
        shaped((len(FIRST_BLOCKS), HALF, COLS), F32),
        (counts, *messages),
        "near_grads",
        flops=1 << 30,
    )
    hop_shapes = (shaped((BLOCK + WROWS, COLS), BF),) * 2
    up0, down0, hubs, skip = call(
        first_grads_kernel,
        (*hop_shapes, shaped((NZ, HUB_ROWS, COLS), F32), shaped((HUB_ROWS, COLS), F32)),
        (counts, *messages, *others, near_grads),
        "first_grads",
        flops=1 << 30,
    )
    up1, down1 = shift(up0, "z", NZ, 1), shift(down0, "z", NZ, -1)
    rests = [
        call(
            functools.partial(rest_grads_kernel, blocks=blocks),
            shaped((2, HALF, COLS), F32),
            (counts, *messages, *others),
            "rest_grads",
            flops=1 << 29,
        )
        for blocks in ((3, 6), (2, 7), (1, 0))
    ]
    skip = shift(skip, "z", NZ, 2)
    ups, downs = [up1], [down1]
    hop_shape, token_shape = shaped((BLOCK + WROWS, COLS), BF), shaped((8, 128), F32)
    token = hubs
    for hub_deltas, rest in zip(((2, 6), (1, 7)), rests):
        for index, (hub_delta, side, step) in enumerate(zip(hub_deltas, (ups, downs), (1, -1))):
            message, token = call(
                functools.partial(hop_kernel, index=index, hub_delta=hub_delta),
                (hop_shape, token_shape),
                (side[-1], rest, hubs, skip, token),
                "hop",
            )
            side.append(shift(message, "z", NZ, step))
    up, token = call(
        last_hop_kernel,
        (shaped((HALF + WROWS, COLS), BF), token_shape),
        (ups[-1], rests[2], token),
        "last_hop",
    )
    hub_sum = call(
        hub_kernel, shaped((HUB_ROWS, COLS), F32), (ups[-1], downs[-1], hubs, token), "hub_sum"
    )
    ups.append(shift(up, "z", NZ, 1))
    hub_sum = lax.ppermute(hub_sum, "x", [(0, 0), (1, 2), (2, 1), (3, 3)])
    grad_features, hub_rows, grad_self, grad_nbr = call(
        final_kernel,
        (
            shaped((HALF, COLS), BF),
            shaped((2 * HUB_ROWS, 64), F32),
            shaped((64, 256), F32),
            shaped((64, 256), F32),
        ),
        (self_term, rests[2], up0, *ups, *downs, hub_sum),
        "last_sums",
        scratch=[pltpu.VMEM((NZ, WROWS, COLS), BF)],
    )
    return outputs, grad_features, hub_rows, grad_self, grad_nbr


def solution(mesh):
    fine = Mesh(mesh.devices.reshape(NY, NZ, NC, NX), ("y", "z", "c", "x"))
    dom = ("y", "z", "c")
    in_specs = (
        P(dom, "x"),
        P(dom, None),
        P(None, dom, None),
        P(None, dom),
        P(dom, None),
        P(),
        P(),
        P(dom, "x"),
    )
    out_specs = (P(dom, "x"), P(dom, "x"), P(dom, "x"), P("x", None), P("x", None))
    return jax.shard_map(body, mesh=fine, in_specs=in_specs, out_specs=out_specs, check_vma=False)
```

profile of v0, /device:TPU:4, one launch (start us, length us, event | category | flops | bytes accessed | tf_op | source)
XLA Modules:
  0.0 97.3 jit_solution(14362366241214456565)
XLA Ops:
  1.9 5.9 %collective-permute-start.6 = (bf16[272,128]{1,0:T(8,128)(2,1)S(1)}, bf16[272,128]{1,0:T(8,128)(2,1)S(1)}, u32[]{:S(2)}, u32[]{:S(2)}) collective-permute-start(bf16[272,128]{1,0:T(8,128)(2,1)S(1)} %get-tuple-element.43.t0), channel_id=1, source_target_pairs={{0,56},{8,0},{16,8},{24,16},{32,24},{40,32},{48,40},{56,48},{1,57}... | collective-permute-start | bytes 208904 | tf_op jit(solution)/shard_map/ppermute | solution.py:33
  10.3 3.3 %collective-permute-start.3 = (s32[2,16,512]{2,1,0:T(8,128)S(1)}, s32[2,16,512]{2,1,0:T(8,128)S(1)}, u32[]{:S(2)}, u32[]{:S(2)}) collective-permute-start(s32[2,16,512]{2,1,0:T(8,128)S(1)} %pad_add_fusion.ids0), channel_id=1, source_target_pairs={{0,128},{64,192},{128,0},{192,64},{1,129},{65,193},{129,1},{193,65... | collective-permute-start | bytes 196616 | tf_op jit(solution)/shard_map/ppermute | solution.py:37
  14.7 1.9 %collective-permute-start.9 = (bf16[544,128]{1,0:T(8,128)(2,1)S(1)}, bf16[544,128]{1,0:T(8,128)(2,1)S(1)}, u32[]{:S(2)}, u32[]{:S(2)}) collective-permute-start(bf16[544,128]{1,0:T(8,128)(2,1)S(1)} %pad_maximum_fusion.1), channel_id=1, source_target_pairs={{0,48},{8,56},{16,0},{24,8},{32,16},{40,24},{48,32},{56,40},{1,49}... | collective-permute-start | bytes 417800 | tf_op jit(solution)/shard_map/ppermute | solution.py:33
  17.9 1.9 %collective-permute-done.5.ids3 = s32[2,16,512]{2,1,0:T(8,128)S(1)} collective-permute-done((s32[2,16,512]{2,1,0:T(8,128)S(1)}, s32[2,16,512]{2,1,0:T(8,128)S(1)}, u32[]{:S(2)}, u32[]{:S(2)}) %collective-permute-start.5) | collective-permute-done | bytes 65568 | tf_op jit(solution)/shard_map/ppermute | solution.py:37
  19.8 8.9 %counts.1 = bf16[8,2304,512]{2,1,0:T(8,128)(2,1)S(1)} custom-call(s32[2,16,512]{2,1,0:T(8,128)S(1)} %pad_add_fusion.ids0, s32[2,16,512]{2,1,0:T(8,128)S(1)} %collective-permute-done.3.ids1, s32[2,16,512]{2,1,0:T(8,128)S(1)} %collective-permute-done.4.ids2, s32[2,16,512]{2,1,0:T(8,128)S(1)} %collective-permute-done.5.ids3), custom_call_target="tpu_custom_call" | custom-call | flops 17179869184 | bytes 262144 | tf_op jit(solution)/shard_map/counts/pallas_call | solution.py:49
  33.2 2.0 %collective-permute-start.12 = (bf16[128,512]{1,0:T(8,128)(2,1)S(1)}, bf16[128,512]{1,0:T(8,128)(2,1)S(1)}, u32[]{:S(2)}, u32[]{:S(2)}) collective-permute-start(bf16[128,512]{1,0:T(8,128)(2,1)S(1)} %get-tuple-element.69), channel_id=1, source_target_pairs={{0,128},{64,192},{128,0},{192,64},{1,129},{65,193},{129,1},{193,65... | collective-permute-start | bytes 393224 | tf_op jit(solution)/shard_map/ppermute | solution.py:37
  35.2 2.2 %collective-permute-start.14 = (bf16[128,512]{1,0:T(8,128)(2,1)S(1)}, bf16[128,512]{1,0:T(8,128)(2,1)S(1)}, u32[]{:S(2)}, u32[]{:S(2)}) collective-permute-start(bf16[128,512]{1,0:T(8,128)(2,1)S(1)} %get-tuple-element.70), channel_id=1, source_target_pairs={{0,192},{64,128},{128,64},{192,0},{1,193},{65,129},{129,65},{193,1... | collective-permute-start | bytes 393224 | tf_op jit(solution)/shard_map/ppermute | solution.py:37
  38.3 2.8 %collective-permute-done.12 = bf16[128,512]{1,0:T(8,128)(2,1)S(1)} collective-permute-done((bf16[128,512]{1,0:T(8,128)(2,1)S(1)}, bf16[128,512]{1,0:T(8,128)(2,1)S(1)}, u32[]{:S(2)}, u32[]{:S(2)}) %collective-permute-start.12) | collective-permute-done | bytes 131104 | tf_op jit(solution)/shard_map/ppermute | solution.py:37
  41.3 1.8 %collective-permute-done.14 = bf16[128,512]{1,0:T(8,128)(2,1)S(1)} collective-permute-done((bf16[128,512]{1,0:T(8,128)(2,1)S(1)}, bf16[128,512]{1,0:T(8,128)(2,1)S(1)}, u32[]{:S(2)}, u32[]{:S(2)}) %collective-permute-start.14) | collective-permute-done | bytes 131104 | tf_op jit(solution)/shard_map/ppermute | solution.py:37
  45.2 2.2 %collective-permute-start.17 = (bf16[128,512]{1,0:T(8,128)(2,1)S(1)}, bf16[128,512]{1,0:T(8,128)(2,1)S(1)}, u32[]{:S(2)}, u32[]{:S(2)}) collective-permute-start(bf16[128,512]{1,0:T(8,128)(2,1)S(1)} %fusion.3.s0), channel_id=1, source_target_pairs={{0,3},{1,2},{2,1},{3,0},{4,7},{5,6},{6,5},{7,4},{8,11},{9,10},{10,... | collective-permute-start | bytes 393224 | tf_op jit(solution)/shard_map/ppermute | solution.py:37
  48.1 3.1 %collective-permute-done.15.s1 = bf16[128,512]{1,0:T(8,128)(2,1)S(1)} collective-permute-done((bf16[128,512]{1,0:T(8,128)(2,1)S(1)}, bf16[128,512]{1,0:T(8,128)(2,1)S(1)}, u32[]{:S(2)}, u32[]{:S(2)}) %collective-permute-start.15) | collective-permute-done | bytes 131104 | tf_op jit(solution)/shard_map/ppermute | solution.py:37
  52.9 1.8 %dense.1 = (bf16[256,128]{1,0:T(8,128)(2,1)}, bf16[768,128]{1,0:T(8,128)(2,1)S(1)}, f32[256,128]{1,0:T(8,128)S(1)}) custom-call(bf16[256,512]{1,0:T(8,128)(2,1)S(1)} %get-tuple-element.37.turned_ref, bf16[512,256]{1,0:T(8,128)(2,1)S(1)} %get-tuple-element.38.cot_ref, f32[512,256]{1,0:T(8,128)S(1)} %get-tuple-element.39.pre_ref, ...), custom_call_target="tpu_custom_call" | custom-call | flops 1073741824 | bytes 262144 | tf_op jit(solution)/shard_map/dense/pallas_call | solution.py:49
  54.7 2.1 %collective-permute-start.18 = (bf16[768,128]{1,0:T(8,128)(2,1)S(1)}, bf16[768,128]{1,0:T(8,128)(2,1)S(1)}, u32[]{:S(2)}, u32[]{:S(2)}) collective-permute-start(bf16[768,128]{1,0:T(8,128)(2,1)S(1)} %get-tuple-element.48.m0), channel_id=1, source_target_pairs={{0,128},{64,192},{128,0},{192,64},{1,129},{65,193},{129,1},{193,65... | collective-permute-start | bytes 589832 | tf_op jit(solution)/shard_map/ppermute | solution.py:37
  56.8 2.0 %collective-permute-start.20 = (bf16[768,128]{1,0:T(8,128)(2,1)S(1)}, bf16[768,128]{1,0:T(8,128)(2,1)S(1)}, u32[]{:S(2)}, u32[]{:S(2)}) collective-permute-start(bf16[768,128]{1,0:T(8,128)(2,1)S(1)} %get-tuple-element.48.m0), channel_id=1, source_target_pairs={{0,192},{64,128},{128,64},{192,0},{1,193},{65,129},{129,65},{193,1... | collective-permute-start | bytes 589832 | tf_op jit(solution)/shard_map/ppermute | solution.py:37
  58.8 5.2 %collective-permute-done.18.m1 = bf16[768,128]{1,0:T(8,128)(2,1)S(1)} collective-permute-done((bf16[768,128]{1,0:T(8,128)(2,1)S(1)}, bf16[768,128]{1,0:T(8,128)(2,1)S(1)}, u32[]{:S(2)}, u32[]{:S(2)}) %collective-permute-start.18) | collective-permute-done | bytes 196640 | tf_op jit(solution)/shard_map/ppermute | solution.py:37
  65.4 1.9 %collective-permute-done.20.m3 = bf16[768,128]{1,0:T(8,128)(2,1)S(1)} collective-permute-done((bf16[768,128]{1,0:T(8,128)(2,1)S(1)}, bf16[768,128]{1,0:T(8,128)(2,1)S(1)}, u32[]{:S(2)}, u32[]{:S(2)}) %collective-permute-start.20) | collective-permute-done | bytes 196640 | tf_op jit(solution)/shard_map/ppermute | solution.py:37
  71.1 3.1 %collective-permute-start.28 = (bf16[528,128]{1,0:T(8,128)(2,1)S(1)}, bf16[528,128]{1,0:T(8,128)(2,1)S(1)}, u32[]{:S(2)}, u32[]{:S(2)}) collective-permute-start(bf16[528,128]{1,0:T(8,128)(2,1)S(1)} %get-tuple-element.53), channel_id=1, source_target_pairs={{0,56},{8,0},{16,8},{24,16},{32,24},{40,32},{48,40},{56,48},{1,57}... | collective-permute-start | bytes 405512 | tf_op jit(solution)/shard_map/ppermute | solution.py:33
  75.5 2.0 %collective-permute-done.26.skip = f32[16,128]{1,0:T(8,128)S(1)} collective-permute-done((f32[16,128]{1,0:T(8,128)S(1)}, f32[16,128]{1,0:T(8,128)S(1)}, u32[]{:S(2)}, u32[]{:S(2)}) %collective-permute-start.26) | collective-permute-done | bytes 8224 | tf_op jit(solution)/shard_map/ppermute | solution.py:33
  78.5 2.4 %collective-permute-start.30 = (bf16[528,128]{1,0:T(8,128)(2,1)S(1)}, bf16[528,128]{1,0:T(8,128)(2,1)S(1)}, u32[]{:S(2)}, u32[]{:S(2)}) collective-permute-start(bf16[528,128]{1,0:T(8,128)(2,1)S(1)} %get-tuple-element.57), channel_id=1, source_target_pairs={{0,56},{8,0},{16,8},{24,16},{32,24},{40,32},{48,40},{56,48},{1,57}... | collective-permute-start | bytes 405512 | tf_op jit(solution)/shard_map/ppermute | solution.py:33
  82.2 1.6 %collective-permute-done.27.got.up2 = bf16[528,128]{1,0:T(8,128)(2,1)S(1)} collective-permute-done((bf16[528,128]{1,0:T(8,128)(2,1)S(1)}, bf16[528,128]{1,0:T(8,128)(2,1)S(1)}, u32[]{:S(2)}, u32[]{:S(2)}) %collective-permute-start.27) | collective-permute-done | bytes 135200 | tf_op jit(solution)/shard_map/ppermute | solution.py:33
  84.0 3.3 %collective-permute-start.32 = (bf16[528,128]{1,0:T(8,128)(2,1)S(1)}, bf16[528,128]{1,0:T(8,128)(2,1)S(1)}, u32[]{:S(2)}, u32[]{:S(2)}) collective-permute-start(bf16[528,128]{1,0:T(8,128)(2,1)S(1)} %get-tuple-element.61), channel_id=1, source_target_pairs={{0,56},{8,0},{16,8},{24,16},{32,24},{40,32},{48,40},{56,48},{1,57}... | collective-permute-start | bytes 405512 | tf_op jit(solution)/shard_map/ppermute | solution.py:33
  88.5 1.6 %collective-permute-done.29.up.up3 = bf16[528,128]{1,0:T(8,128)(2,1)S(1)} collective-permute-done((bf16[528,128]{1,0:T(8,128)(2,1)S(1)}, bf16[528,128]{1,0:T(8,128)(2,1)S(1)}, u32[]{:S(2)}, u32[]{:S(2)}) %collective-permute-start.29) | collective-permute-done | bytes 135200 | tf_op jit(solution)/shard_map/ppermute | solution.py:33
  90.3 1.9 %collective-permute-start.33 = (f32[16,128]{1,0:T(8,128)S(1)}, f32[16,128]{1,0:T(8,128)S(1)}, u32[]{:S(2)}, u32[]{:S(2)}) collective-permute-start(f32[16,128]{1,0:T(8,128)S(1)} %hub_sum.1), channel_id=1, source_target_pairs={{0,0},{1,2},{2,1},{3,3},{4,4},{5,6},{6,5},{7,7},{8,8},{9,10},{10,9... | collective-permute-start | bytes 24584 | tf_op jit(solution)/shard_map/ppermute | solution.py:490
  92.2 3.6 %collective-permute-done.33.hub_sum = f32[16,128]{1,0:T(8,128)S(1)} collective-permute-done((f32[16,128]{1,0:T(8,128)S(1)}, f32[16,128]{1,0:T(8,128)S(1)}, u32[]{:S(2)}, u32[]{:S(2)}) %collective-permute-start.33) | collective-permute-done | bytes 8224 | tf_op jit(solution)/shard_map/ppermute | solution.py:490
  (73 shorter events, 27.9 us)
Async XLA Ops:
  1.8 8.5 %collective-permute-start.2 = (s32[16,512]{1,0:T(8,128)S(1)}, s32[16,512]{1,0:T(8,128)S(1)}, u32[]{:S(2)}, u32[]{:S(2)}) collective-permute-start(s32[16,512]{1,0:T(8,128)S(1)} %get-tuple-element.42), channel_id=1, source_target_pairs={{0,4},{4,0},{1,5},{5,1},{2,6},{6,2},{3,7},{7,3},{8,12},{12,8},{9,1... | collective-permute-start | bytes 98312 | tf_op jit(solution)/shard_map/ppermute | solution.py:37
  1.9 12.4 %collective-permute-start.6 = (bf16[272,128]{1,0:T(8,128)(2,1)S(1)}, bf16[272,128]{1,0:T(8,128)(2,1)S(1)}, u32[]{:S(2)}, u32[]{:S(2)}) collective-permute-start(bf16[272,128]{1,0:T(8,128)(2,1)S(1)} %get-tuple-element.43.t0), channel_id=1, source_target_pairs={{0,56},{8,0},{16,8},{24,16},{32,24},{40,32},{48,40},{56,48},{1,57}... | collective-permute-start | bytes 208904 | tf_op jit(solution)/shard_map/ppermute | solution.py:33
  7.8 6.8 %collective-permute-start.7 = (bf16[272,128]{1,0:T(8,128)(2,1)S(1)}, bf16[272,128]{1,0:T(8,128)(2,1)S(1)}, u32[]{:S(2)}, u32[]{:S(2)}) collective-permute-start(bf16[272,128]{1,0:T(8,128)(2,1)S(1)} %get-tuple-element.43.t0), channel_id=1, source_target_pairs={{0,48},{8,56},{16,0},{24,8},{32,16},{40,24},{48,32},{56,40},{1,49}... | collective-permute-start | bytes 208904 | tf_op jit(solution)/shard_map/ppermute | solution.py:33
  9.3 7.3 %collective-permute-start.8 = (bf16[272,128]{1,0:T(8,128)(2,1)S(1)}, bf16[272,128]{1,0:T(8,128)(2,1)S(1)}, u32[]{:S(2)}, u32[]{:S(2)}) collective-permute-start(bf16[272,128]{1,0:T(8,128)(2,1)S(1)} %get-tuple-element.43.t0), channel_id=1, source_target_pairs={{0,8},{8,16},{16,24},{24,32},{32,40},{40,48},{48,56},{56,0},{1,9},... | collective-permute-start | bytes 208904 | tf_op jit(solution)/shard_map/ppermute | solution.py:33
  10.3 7.5 %collective-permute-start.3 = (s32[2,16,512]{2,1,0:T(8,128)S(1)}, s32[2,16,512]{2,1,0:T(8,128)S(1)}, u32[]{:S(2)}, u32[]{:S(2)}) collective-permute-start(s32[2,16,512]{2,1,0:T(8,128)S(1)} %pad_add_fusion.ids0), channel_id=1, source_target_pairs={{0,128},{64,192},{128,0},{192,64},{1,129},{65,193},{129,1},{193,65... | collective-permute-start | bytes 196616 | tf_op jit(solution)/shard_map/ppermute | solution.py:37
  14.7 14.0 %collective-permute-start.9 = (bf16[544,128]{1,0:T(8,128)(2,1)S(1)}, bf16[544,128]{1,0:T(8,128)(2,1)S(1)}, u32[]{:S(2)}, u32[]{:S(2)}) collective-permute-start(bf16[544,128]{1,0:T(8,128)(2,1)S(1)} %pad_maximum_fusion.1), channel_id=1, source_target_pairs={{0,48},{8,56},{16,0},{24,8},{32,16},{40,24},{48,32},{56,40},{1,49}... | collective-permute-start | bytes 417800 | tf_op jit(solution)/shard_map/ppermute | solution.py:33
  16.6 12.1 %collective-permute-start.10 = (bf16[544,128]{1,0:T(8,128)(2,1)S(1)}, bf16[544,128]{1,0:T(8,128)(2,1)S(1)}, u32[]{:S(2)}, u32[]{:S(2)}) collective-permute-start(bf16[544,128]{1,0:T(8,128)(2,1)S(1)} %pad_maximum_fusion.2), channel_id=1, source_target_pairs={{0,16},{8,24},{16,32},{24,40},{32,48},{40,56},{48,0},{56,8},{1,17}... | collective-permute-start | bytes 417800 | tf_op jit(solution)/shard_map/ppermute | solution.py:33
  30.2 7.1 %collective-permute-start = (bf16[512,128]{1,0:T(8,128)(2,1)S(1)}, bf16[512,128]{1,0:T(8,128)(2,1)S(1)}, u32[]{:S(2)}, u32[]{:S(2)}) collective-permute-start(bf16[512,128]{1,0:T(8,128)(2,1)S(1)} %get-tuple-element.36.fg0), channel_id=1, source_target_pairs={{0,1},{1,0},{2,3},{3,2},{4,5},{5,4},{6,7},{7,6},{8,9},{9,8},{10,11... | collective-permute-start | bytes 393224 | tf_op jit(solution)/shard_map/ppermute | solution.py:37
  33.2 7.9 %collective-permute-start.12 = (bf16[128,512]{1,0:T(8,128)(2,1)S(1)}, bf16[128,512]{1,0:T(8,128)(2,1)S(1)}, u32[]{:S(2)}, u32[]{:S(2)}) collective-permute-start(bf16[128,512]{1,0:T(8,128)(2,1)S(1)} %get-tuple-element.69), channel_id=1, source_target_pairs={{0,128},{64,192},{128,0},{192,64},{1,129},{65,193},{129,1},{193,65... | collective-permute-start | bytes 393224 | tf_op jit(solution)/shard_map/ppermute | solution.py:37
  35.2 7.9 %collective-permute-start.14 = (bf16[128,512]{1,0:T(8,128)(2,1)S(1)}, bf16[128,512]{1,0:T(8,128)(2,1)S(1)}, u32[]{:S(2)}, u32[]{:S(2)}) collective-permute-start(bf16[128,512]{1,0:T(8,128)(2,1)S(1)} %get-tuple-element.70), channel_id=1, source_target_pairs={{0,192},{64,128},{128,64},{192,0},{1,193},{65,129},{129,65},{193,1... | collective-permute-start | bytes 393224 | tf_op jit(solution)/shard_map/ppermute | solution.py:37
  37.4 10.0 %collective-permute-start.1 = (bf16[1024,128]{1,0:T(8,128)(2,1)S(1)}, bf16[1024,128]{1,0:T(8,128)(2,1)S(1)}, u32[]{:S(2)}, u32[]{:S(2)}) collective-permute-start(bf16[1024,128]{1,0:T(8,128)(2,1)S(1)} %pad_maximum_fusion), channel_id=1, source_target_pairs={{0,2},{1,3},{2,0},{3,1},{4,6},{5,7},{6,4},{7,5},{8,10},{9,11},{10,... | collective-permute-start | bytes 786440 | tf_op jit(solution)/shard_map/ppermute | solution.py:37
  43.2 8.0 %collective-permute-start.15 = (bf16[128,512]{1,0:T(8,128)(2,1)S(1)}, bf16[128,512]{1,0:T(8,128)(2,1)S(1)}, u32[]{:S(2)}, u32[]{:S(2)}) collective-permute-start(bf16[128,512]{1,0:T(8,128)(2,1)S(1)} %fusion.3.s0), channel_id=1, source_target_pairs={{0,2},{1,3},{2,0},{3,1},{4,6},{5,7},{6,4},{7,5},{8,10},{9,11},{10,... | collective-permute-start | bytes 393224 | tf_op jit(solution)/shard_map/ppermute | solution.py:37
  44.1 7.2 %collective-permute-start.16 = (bf16[128,512]{1,0:T(8,128)(2,1)S(1)}, bf16[128,512]{1,0:T(8,128)(2,1)S(1)}, u32[]{:S(2)}, u32[]{:S(2)}) collective-permute-start(bf16[128,512]{1,0:T(8,128)(2,1)S(1)} %fusion.3.s0), channel_id=1, source_target_pairs={{0,1},{1,0},{2,3},{3,2},{4,5},{5,4},{6,7},{7,6},{8,9},{9,8},{10,11... | collective-permute-start | bytes 393224 | tf_op jit(solution)/shard_map/ppermute | solution.py:37
  45.2 7.7 %collective-permute-start.17 = (bf16[128,512]{1,0:T(8,128)(2,1)S(1)}, bf16[128,512]{1,0:T(8,128)(2,1)S(1)}, u32[]{:S(2)}, u32[]{:S(2)}) collective-permute-start(bf16[128,512]{1,0:T(8,128)(2,1)S(1)} %fusion.3.s0), channel_id=1, source_target_pairs={{0,3},{1,2},{2,1},{3,0},{4,7},{5,6},{6,5},{7,4},{8,11},{9,10},{10,... | collective-permute-start | bytes 393224 | tf_op jit(solution)/shard_map/ppermute | solution.py:37
  54.7 9.3 %collective-permute-start.18 = (bf16[768,128]{1,0:T(8,128)(2,1)S(1)}, bf16[768,128]{1,0:T(8,128)(2,1)S(1)}, u32[]{:S(2)}, u32[]{:S(2)}) collective-permute-start(bf16[768,128]{1,0:T(8,128)(2,1)S(1)} %get-tuple-element.48.m0), channel_id=1, source_target_pairs={{0,128},{64,192},{128,0},{192,64},{1,129},{65,193},{129,1},{193,65... | collective-permute-start | bytes 589832 | tf_op jit(solution)/shard_map/ppermute | solution.py:37
  56.8 8.6 %collective-permute-start.19 = (bf16[768,128]{1,0:T(8,128)(2,1)S(1)}, bf16[768,128]{1,0:T(8,128)(2,1)S(1)}, u32[]{:S(2)}, u32[]{:S(2)}) collective-permute-start(bf16[768,128]{1,0:T(8,128)(2,1)S(1)} %get-tuple-element.48.m0), channel_id=1, source_target_pairs={{0,64},{64,0},{128,192},{192,128},{1,65},{65,1},{129,193},{193,129... | collective-permute-start | bytes 589832 | tf_op jit(solution)/shard_map/ppermute | solution.py:37
  56.8 10.5 %collective-permute-start.20 = (bf16[768,128]{1,0:T(8,128)(2,1)S(1)}, bf16[768,128]{1,0:T(8,128)(2,1)S(1)}, u32[]{:S(2)}, u32[]{:S(2)}) collective-permute-start(bf16[768,128]{1,0:T(8,128)(2,1)S(1)} %get-tuple-element.48.m0), channel_id=1, source_target_pairs={{0,192},{64,128},{128,64},{192,0},{1,193},{65,129},{129,65},{193,1... | collective-permute-start | bytes 589832 | tf_op jit(solution)/shard_map/ppermute | solution.py:37
  58.8 9.4 %collective-permute-start.21 = (bf16[768,128]{1,0:T(8,128)(2,1)S(1)}, bf16[768,128]{1,0:T(8,128)(2,1)S(1)}, u32[]{:S(2)}, u32[]{:S(2)}) collective-permute-start(bf16[768,128]{1,0:T(8,128)(2,1)S(1)} %get-tuple-element.48.m0), channel_id=1, source_target_pairs={{0,4},{4,0},{1,5},{5,1},{2,6},{6,2},{3,7},{7,3},{8,12},{12,8},{9,1... | collective-permute-start | bytes 589832 | tf_op jit(solution)/shard_map/ppermute | solution.py:37
  69.8 7.7 %collective-permute-start.25 = (bf16[528,128]{1,0:T(8,128)(2,1)S(1)}, bf16[528,128]{1,0:T(8,128)(2,1)S(1)}, u32[]{:S(2)}, u32[]{:S(2)}) collective-permute-start(bf16[528,128]{1,0:T(8,128)(2,1)S(1)} %get-tuple-element.49.first), channel_id=1, source_target_pairs={{0,8},{8,16},{16,24},{24,32},{32,40},{40,48},{48,56},{56,0},{1,9},... | collective-permute-start | bytes 405512 | tf_op jit(solution)/shard_map/ppermute | solution.py:33
  70.3 7.2 %collective-permute-start.26 = (f32[16,128]{1,0:T(8,128)S(1)}, f32[16,128]{1,0:T(8,128)S(1)}, u32[]{:S(2)}, u32[]{:S(2)}) collective-permute-start(f32[16,128]{1,0:T(8,128)S(1)} %get-tuple-element.51), channel_id=1, source_target_pairs={{0,16},{8,24},{16,32},{24,40},{32,48},{40,56},{48,0},{56,8},{1,17}... | collective-permute-start | bytes 24584 | tf_op jit(solution)/shard_map/ppermute | solution.py:33
  71.1 7.4 %collective-permute-start.28 = (bf16[528,128]{1,0:T(8,128)(2,1)S(1)}, bf16[528,128]{1,0:T(8,128)(2,1)S(1)}, u32[]{:S(2)}, u32[]{:S(2)}) collective-permute-start(bf16[528,128]{1,0:T(8,128)(2,1)S(1)} %get-tuple-element.53), channel_id=1, source_target_pairs={{0,56},{8,0},{16,8},{24,16},{32,24},{40,32},{48,40},{56,48},{1,57}... | collective-permute-start | bytes 405512 | tf_op jit(solution)/shard_map/ppermute | solution.py:33
  77.5 6.3 %collective-permute-start.27 = (bf16[528,128]{1,0:T(8,128)(2,1)S(1)}, bf16[528,128]{1,0:T(8,128)(2,1)S(1)}, u32[]{:S(2)}, u32[]{:S(2)}) collective-permute-start(bf16[528,128]{1,0:T(8,128)(2,1)S(1)} %get-tuple-element.52), channel_id=1, source_target_pairs={{0,8},{8,16},{16,24},{24,32},{32,40},{40,48},{48,56},{56,0},{1,9},... | collective-permute-start | bytes 405512 | tf_op jit(solution)/shard_map/ppermute | solution.py:33
  83.8 6.3 %collective-permute-start.29 = (bf16[528,128]{1,0:T(8,128)(2,1)S(1)}, bf16[528,128]{1,0:T(8,128)(2,1)S(1)}, u32[]{:S(2)}, u32[]{:S(2)}) collective-permute-start(bf16[528,128]{1,0:T(8,128)(2,1)S(1)} %get-tuple-element.56), channel_id=1, source_target_pairs={{0,8},{8,16},{16,24},{24,32},{32,40},{40,48},{48,56},{56,0},{1,9},... | collective-permute-start | bytes 405512 | tf_op jit(solution)/shard_map/ppermute | solution.py:33
  84.0 6.3 %collective-permute-start.32 = (bf16[528,128]{1,0:T(8,128)(2,1)S(1)}, bf16[528,128]{1,0:T(8,128)(2,1)S(1)}, u32[]{:S(2)}, u32[]{:S(2)}) collective-permute-start(bf16[528,128]{1,0:T(8,128)(2,1)S(1)} %get-tuple-element.61), channel_id=1, source_target_pairs={{0,56},{8,0},{16,8},{24,16},{32,24},{40,32},{48,40},{56,48},{1,57}... | collective-permute-start | bytes 405512 | tf_op jit(solution)/shard_map/ppermute | solution.py:33
  (12 other events, 87.4 us)
where the time goes:
time: 98.2 us; the launch traced here: 97.3 us
  starting transfers between devices  43.9 us (45%)
  waiting for transfers between devices  30 us (31%)
  Pallas kernels  22.1 us (23%)
    ppermute x13, starting transfers between devices, shift(): return lax.ppermute(x, axis, [(i, (i + step) % size) for i in range(size)])  22.8 us
    pallas_call x18, Pallas kernels, call(): pl.pallas_call(kernel, out_shape=outs, in_specs=[VM] * (len(inputs) - far...  22.1 us
    ppermute x20, waiting for transfers between devices, swap(): return lax.ppermute(x, axis, [(i, i ^ mask) for i in range(size)])  20.5 us
    ppermute x20, starting transfers between devices, swap(): return lax.ppermute(x, axis, [(i, i ^ mask) for i in range(size)])  19.2 us
    ppermute x13, waiting for transfers between devices, shift(): return lax.ppermute(x, axis, [(i, (i + step) % size) for i in range(size)])  5.85 us
    ppermute x1, waiting for transfers between devices, body(): hub_sum = lax.ppermute(hub_sum, 'x', [(0, 0), (1, 2), (2, 1), (3, 3)])  3.62 us
  transfers between devices with their start and end apart: 34, of which 17 were waited for; matrix products, arithmetic and copies ran while one was open for 0% of the time, Pallas kernels for 16%

commit v1 on v0

--- a/solution.py
+++ b/solution.py
@@ -91,7 +91,7 @@
     mine_ref[HALF:BLOCK] = dot(pick.astype(F32).astype(BF), columns).astype(BF)
 
 
-def counts_kernel(ids0, ids1, ids2, ids3, out_ref, ids_scr, key_scr):
+def counts_kernel(ids0, ids1, ids2, ids3, out_ref, ids_scr):
     y, z, c, x = (lax.axis_index(a) for a in ("y", "z", "c", "x"))
     parity = x // 2
     rows = lax.broadcasted_iota(jnp.int32, (16, 16, 128), 0) * 16 + lax.broadcasted_iota(
@@ -155,20 +155,14 @@
 
         def more(keys):
             keys, top, times = extract(keys)
-            key_scr[0] = top
-            key_scr[1] = times
-
-            def fix(step, inner):
-                delta = step % NZ
-                lanes = pl.ds(pl.multiple_of(step // NZ * 128, 128), 128)
-                span = pl.ds(pl.multiple_of(delta * HALF, HALF), HALF)
-                wanted = key_scr[0, :, lanes] - (delta * HALF).astype(F32)
-                block = out_ref[index, span, lanes].reshape(16, 16, 128)
-                block = jnp.where(pair(wanted)[None] == rows, pair(key_scr[1, :, lanes])[None], block)
-                out_ref[index, span, lanes] = block.reshape(HALF, 128)
-                return inner
-
-            lax.fori_loop(0, NZ * (V // 128), fix, 0)
+            for tile in range(V // 128):
+                lanes = slice(tile * 128, (tile + 1) * 128)
+                for delta in range(NZ):
+                    span = slice(delta * HALF, (delta + 1) * HALF)
+                    block = out_ref[index, span, lanes].reshape(16, 16, 128)
+                    match = pair(top[:, lanes] - float(HALF * delta))[None] == rows
+                    block = jnp.where(match, pair(times[:, lanes])[None], block)
+                    out_ref[index, span, lanes] = block.reshape(HALF, 128)
             return keys
 
         lax.while_loop(lambda keys: jnp.max(keys) >= 0, more, keys)
@@ -388,7 +382,7 @@
         (*pairs,),
         "counts",
         flops=1 << 34,
-        scratch=[pltpu.VMEM((PARTS, 16, V), jnp.int32), pltpu.VMEM((2, 8, V), F32)],
+        scratch=[pltpu.VMEM((PARTS, 16, V), jnp.int32)],
         mib=8,
     )
 

time: 98.2 us -> 97.9 us (level)
    ppermute x13, starting transfers between devices: 22.8 us -> 21.7 us  [shift(): return lax.ppermute(x, axis, [(i, (i + step) % size) for i in range(size)])]
where the time goes in v1:
time: 97.9 us; the launch traced here: 97.1 us
  starting transfers between devices  43.4 us (44%)
  waiting for transfers between devices  30.3 us (31%)
  Pallas kernels  22.1 us (23%)
    pallas_call x18, Pallas kernels, call(): pl.pallas_call(kernel, out_shape=outs, in_specs=[VM] * (len(inputs) - far...  22.1 us
    ppermute x13, starting transfers between devices, shift(): return lax.ppermute(x, axis, [(i, (i + step) % size) for i in range(size)])  21.7 us
    ppermute x20, waiting for transfers between devices, swap(): return lax.ppermute(x, axis, [(i, i ^ mask) for i in range(size)])  19.9 us
    ppermute x20, starting transfers between devices, swap(): return lax.ppermute(x, axis, [(i, i ^ mask) for i in range(size)])  19.8 us
    ppermute x13, waiting for transfers between devices, shift(): return lax.ppermute(x, axis, [(i, (i + step) % size) for i in range(size)])  6.72 us
    ppermute x1, waiting for transfers between devices, body(): hub_sum = lax.ppermute(hub_sum, 'x', [(0, 0), (1, 2), (2, 1), (3, 3)])  3.62 us
  transfers between devices with their start and end apart: 34, of which 17 were waited for; matrix products, arithmetic and copies ran while one was open for 0% of the time, Pallas kernels for 16%

profile of v1, /device:TPU:4, one launch (start us, length us, event | category | flops | bytes accessed | tf_op | source)
XLA Modules:
  0.0 97.1 jit_solution(5964841347386734303)
XLA Ops:
  1.9 5.9 %collective-permute-start.6 = (bf16[272,128]{1,0:T(8,128)(2,1)S(1)}, bf16[272,128]{1,0:T(8,128)(2,1)S(1)}, u32[]{:S(2)}, u32[]{:S(2)}) collective-permute-start(bf16[272,128]{1,0:T(8,128)(2,1)S(1)} %get-tuple-element.43.t0), channel_id=1, source_target_pairs={{0,56},{8,0},{16,8},{24,16},{32,24},{40,32},{48,40},{56,48},{1,57}... | collective-permute-start | bytes 208904 | tf_op jit(solution)/shard_map/ppermute | solution.py:33
  7.8 1.5 %collective-permute-start.7 = (bf16[272,128]{1,0:T(8,128)(2,1)S(1)}, bf16[272,128]{1,0:T(8,128)(2,1)S(1)}, u32[]{:S(2)}, u32[]{:S(2)}) collective-permute-start(bf16[272,128]{1,0:T(8,128)(2,1)S(1)} %get-tuple-element.43.t0), channel_id=1, source_target_pairs={{0,48},{8,56},{16,0},{24,8},{32,16},{40,24},{48,32},{56,40},{1,49}... | collective-permute-start | bytes 208904 | tf_op jit(solution)/shard_map/ppermute | solution.py:33
  10.3 3.3 %collective-permute-start.3 = (s32[2,16,512]{2,1,0:T(8,128)S(1)}, s32[2,16,512]{2,1,0:T(8,128)S(1)}, u32[]{:S(2)}, u32[]{:S(2)}) collective-permute-start(s32[2,16,512]{2,1,0:T(8,128)S(1)} %pad_add_fusion.ids0), channel_id=1, source_target_pairs={{0,128},{64,192},{128,0},{192,64},{1,129},{65,193},{129,1},{193,65... | collective-permute-start | bytes 196616 | tf_op jit(solution)/shard_map/ppermute | solution.py:37
  14.7 1.9 %collective-permute-start.9 = (bf16[544,128]{1,0:T(8,128)(2,1)S(1)}, bf16[544,128]{1,0:T(8,128)(2,1)S(1)}, u32[]{:S(2)}, u32[]{:S(2)}) collective-permute-start(bf16[544,128]{1,0:T(8,128)(2,1)S(1)} %pad_maximum_fusion.1), channel_id=1, source_target_pairs={{0,48},{8,56},{16,0},{24,8},{32,16},{40,24},{48,32},{56,40},{1,49}... | collective-permute-start | bytes 417800 | tf_op jit(solution)/shard_map/ppermute | solution.py:33
  17.9 1.9 %collective-permute-done.5.ids3 = s32[2,16,512]{2,1,0:T(8,128)S(1)} collective-permute-done((s32[2,16,512]{2,1,0:T(8,128)S(1)}, s32[2,16,512]{2,1,0:T(8,128)S(1)}, u32[]{:S(2)}, u32[]{:S(2)}) %collective-permute-start.5) | collective-permute-done | bytes 65568 | tf_op jit(solution)/shard_map/ppermute | solution.py:37
  19.8 8.9 %counts.1 = bf16[8,2304,512]{2,1,0:T(8,128)(2,1)S(1)} custom-call(s32[2,16,512]{2,1,0:T(8,128)S(1)} %pad_add_fusion.ids0, s32[2,16,512]{2,1,0:T(8,128)S(1)} %collective-permute-done.3.ids1, s32[2,16,512]{2,1,0:T(8,128)S(1)} %collective-permute-done.4.ids2, s32[2,16,512]{2,1,0:T(8,128)S(1)} %collective-permute-done.5.ids3), custom_call_target="tpu_custom_call" | custom-call | flops 17179869184 | bytes 262144 | tf_op jit(solution)/shard_map/counts/pallas_call | solution.py:49
  28.7 1.4 %far_sums.1 = (bf16[4,128,512]{2,1,0:T(8,128)(2,1)S(1)}, bf16[128,2304]{1,0:T(8,128)(2,1)S(1)}) custom-call(bf16[8,2304,512]{2,1,0:T(8,128)(2,1)S(1)} %counts.1, bf16[272,128]{1,0:T(8,128)(2,1)S(1)} %get-tuple-element.43.t0, bf16[272,128]{1,0:T(8,128)(2,1)S(1)} %collective-permute-done.6.t1, bf16[272,128]{1,0:T(8,128)(2,1)S(1)} %collective-permute-done.7.t2, ...), custom_call_target="tpu_custom_call" | custom-call | flops 2147483648 | bytes 262144 | tf_op jit(solution)/shard_map/far_sums/pallas_call | solution.py:49
  35.0 2.3 %collective-permute-start.14 = (bf16[128,512]{1,0:T(8,128)(2,1)S(1)}, bf16[128,512]{1,0:T(8,128)(2,1)S(1)}, u32[]{:S(2)}, u32[]{:S(2)}) collective-permute-start(bf16[128,512]{1,0:T(8,128)(2,1)S(1)} %get-tuple-element.70), channel_id=1, source_target_pairs={{0,192},{64,128},{128,64},{192,0},{1,193},{65,129},{129,65},{193,1... | collective-permute-start | bytes 393224 | tf_op jit(solution)/shard_map/ppermute | solution.py:37
  38.8 2.3 %collective-permute-done.12 = bf16[128,512]{1,0:T(8,128)(2,1)S(1)} collective-permute-done((bf16[128,512]{1,0:T(8,128)(2,1)S(1)}, bf16[128,512]{1,0:T(8,128)(2,1)S(1)}, u32[]{:S(2)}, u32[]{:S(2)}) %collective-permute-start.12) | collective-permute-done | bytes 131104 | tf_op jit(solution)/shard_map/ppermute | solution.py:37
  41.3 1.8 %collective-permute-done.14 = bf16[128,512]{1,0:T(8,128)(2,1)S(1)} collective-permute-done((bf16[128,512]{1,0:T(8,128)(2,1)S(1)}, bf16[128,512]{1,0:T(8,128)(2,1)S(1)}, u32[]{:S(2)}, u32[]{:S(2)}) %collective-permute-start.14) | collective-permute-done | bytes 131104 | tf_op jit(solution)/shard_map/ppermute | solution.py:37
  45.7 1.7 %collective-permute-start.17 = (bf16[128,512]{1,0:T(8,128)(2,1)S(1)}, bf16[128,512]{1,0:T(8,128)(2,1)S(1)}, u32[]{:S(2)}, u32[]{:S(2)}) collective-permute-start(bf16[128,512]{1,0:T(8,128)(2,1)S(1)} %fusion.3.s0), channel_id=1, source_target_pairs={{0,3},{1,2},{2,1},{3,0},{4,7},{5,6},{6,5},{7,4},{8,11},{9,10},{10,... | collective-permute-start | bytes 393224 | tf_op jit(solution)/shard_map/ppermute | solution.py:37
  48.1 3.1 %collective-permute-done.15.s1 = bf16[128,512]{1,0:T(8,128)(2,1)S(1)} collective-permute-done((bf16[128,512]{1,0:T(8,128)(2,1)S(1)}, bf16[128,512]{1,0:T(8,128)(2,1)S(1)}, u32[]{:S(2)}, u32[]{:S(2)}) %collective-permute-start.15) | collective-permute-done | bytes 131104 | tf_op jit(solution)/shard_map/ppermute | solution.py:37
  53.0 1.8 %dense.1 = (bf16[256,128]{1,0:T(8,128)(2,1)}, bf16[768,128]{1,0:T(8,128)(2,1)S(1)}, f32[256,128]{1,0:T(8,128)S(1)}) custom-call(bf16[256,512]{1,0:T(8,128)(2,1)S(1)} %get-tuple-element.37.turned_ref, bf16[512,256]{1,0:T(8,128)(2,1)S(1)} %get-tuple-element.38.cot_ref, f32[512,256]{1,0:T(8,128)S(1)} %get-tuple-element.39.pre_ref, ...), custom_call_target="tpu_custom_call" | custom-call | flops 1073741824 | bytes 262144 | tf_op jit(solution)/shard_map/dense/pallas_call | solution.py:49
  56.0 2.9 %collective-permute-start.20 = (bf16[768,128]{1,0:T(8,128)(2,1)S(1)}, bf16[768,128]{1,0:T(8,128)(2,1)S(1)}, u32[]{:S(2)}, u32[]{:S(2)}) collective-permute-start(bf16[768,128]{1,0:T(8,128)(2,1)S(1)} %get-tuple-element.48.m0), channel_id=1, source_target_pairs={{0,192},{64,128},{128,64},{192,0},{1,193},{65,129},{129,65},{193,1... | collective-permute-start | bytes 589832 | tf_op jit(solution)/shard_map/ppermute | solution.py:37
  58.9 5.2 %collective-permute-done.18.m1 = bf16[768,128]{1,0:T(8,128)(2,1)S(1)} collective-permute-done((bf16[768,128]{1,0:T(8,128)(2,1)S(1)}, bf16[768,128]{1,0:T(8,128)(2,1)S(1)}, u32[]{:S(2)}, u32[]{:S(2)}) %collective-permute-start.18) | collective-permute-done | bytes 196640 | tf_op jit(solution)/shard_map/ppermute | solution.py:37
  64.6 2.7 %collective-permute-done.20.m3 = bf16[768,128]{1,0:T(8,128)(2,1)S(1)} collective-permute-done((bf16[768,128]{1,0:T(8,128)(2,1)S(1)}, bf16[768,128]{1,0:T(8,128)(2,1)S(1)}, u32[]{:S(2)}, u32[]{:S(2)}) %collective-permute-start.20) | collective-permute-done | bytes 196640 | tf_op jit(solution)/shard_map/ppermute | solution.py:37
  71.4 1.8 %collective-permute-start.28 = (bf16[528,128]{1,0:T(8,128)(2,1)S(1)}, bf16[528,128]{1,0:T(8,128)(2,1)S(1)}, u32[]{:S(2)}, u32[]{:S(2)}) collective-permute-start(bf16[528,128]{1,0:T(8,128)(2,1)S(1)} %get-tuple-element.53), channel_id=1, source_target_pairs={{0,56},{8,0},{16,8},{24,16},{32,24},{40,32},{48,40},{56,48},{1,57}... | collective-permute-start | bytes 405512 | tf_op jit(solution)/shard_map/ppermute | solution.py:33
  74.4 2.8 %collective-permute-done.26.skip = f32[16,128]{1,0:T(8,128)S(1)} collective-permute-done((f32[16,128]{1,0:T(8,128)S(1)}, f32[16,128]{1,0:T(8,128)S(1)}, u32[]{:S(2)}, u32[]{:S(2)}) %collective-permute-start.26) | collective-permute-done | bytes 8224 | tf_op jit(solution)/shard_map/ppermute | solution.py:33
  78.6 2.1 %collective-permute-start.30 = (bf16[528,128]{1,0:T(8,128)(2,1)S(1)}, bf16[528,128]{1,0:T(8,128)(2,1)S(1)}, u32[]{:S(2)}, u32[]{:S(2)}) collective-permute-start(bf16[528,128]{1,0:T(8,128)(2,1)S(1)} %get-tuple-element.57), channel_id=1, source_target_pairs={{0,56},{8,0},{16,8},{24,16},{32,24},{40,32},{48,40},{56,48},{1,57}... | collective-permute-start | bytes 405512 | tf_op jit(solution)/shard_map/ppermute | solution.py:33
  82.0 1.6 %collective-permute-done.27.got.up2 = bf16[528,128]{1,0:T(8,128)(2,1)S(1)} collective-permute-done((bf16[528,128]{1,0:T(8,128)(2,1)S(1)}, bf16[528,128]{1,0:T(8,128)(2,1)S(1)}, u32[]{:S(2)}, u32[]{:S(2)}) %collective-permute-start.27) | collective-permute-done | bytes 135200 | tf_op jit(solution)/shard_map/ppermute | solution.py:33
  83.8 3.3 %collective-permute-start.32 = (bf16[528,128]{1,0:T(8,128)(2,1)S(1)}, bf16[528,128]{1,0:T(8,128)(2,1)S(1)}, u32[]{:S(2)}, u32[]{:S(2)}) collective-permute-start(bf16[528,128]{1,0:T(8,128)(2,1)S(1)} %get-tuple-element.61), channel_id=1, source_target_pairs={{0,56},{8,0},{16,8},{24,16},{32,24},{40,32},{48,40},{56,48},{1,57}... | collective-permute-start | bytes 405512 | tf_op jit(solution)/shard_map/ppermute | solution.py:33
  88.3 1.6 %collective-permute-done.29.up.up3 = bf16[528,128]{1,0:T(8,128)(2,1)S(1)} collective-permute-done((bf16[528,128]{1,0:T(8,128)(2,1)S(1)}, bf16[528,128]{1,0:T(8,128)(2,1)S(1)}, u32[]{:S(2)}, u32[]{:S(2)}) %collective-permute-start.29) | collective-permute-done | bytes 135200 | tf_op jit(solution)/shard_map/ppermute | solution.py:33
  90.1 1.9 %collective-permute-start.33 = (f32[16,128]{1,0:T(8,128)S(1)}, f32[16,128]{1,0:T(8,128)S(1)}, u32[]{:S(2)}, u32[]{:S(2)}) collective-permute-start(f32[16,128]{1,0:T(8,128)S(1)} %hub_sum.1), channel_id=1, source_target_pairs={{0,0},{1,2},{2,1},{3,3},{4,4},{5,6},{6,5},{7,7},{8,8},{9,10},{10,9... | collective-permute-start | bytes 24584 | tf_op jit(solution)/shard_map/ppermute | solution.py:484
  92.0 3.6 %collective-permute-done.33.hub_sum = f32[16,128]{1,0:T(8,128)S(1)} collective-permute-done((f32[16,128]{1,0:T(8,128)S(1)}, f32[16,128]{1,0:T(8,128)S(1)}, u32[]{:S(2)}, u32[]{:S(2)}) %collective-permute-start.33) | collective-permute-done | bytes 8224 | tf_op jit(solution)/shard_map/ppermute | solution.py:484
  (73 shorter events, 28.8 us)
Async XLA Ops:
  1.8 8.5 %collective-permute-start.2 = (s32[16,512]{1,0:T(8,128)S(1)}, s32[16,512]{1,0:T(8,128)S(1)}, u32[]{:S(2)}, u32[]{:S(2)}) collective-permute-start(s32[16,512]{1,0:T(8,128)S(1)} %get-tuple-element.42), channel_id=1, source_target_pairs={{0,4},{4,0},{1,5},{5,1},{2,6},{6,2},{3,7},{7,3},{8,12},{12,8},{9,1... | collective-permute-start | bytes 98312 | tf_op jit(solution)/shard_map/ppermute | solution.py:37
  1.9 12.4 %collective-permute-start.6 = (bf16[272,128]{1,0:T(8,128)(2,1)S(1)}, bf16[272,128]{1,0:T(8,128)(2,1)S(1)}, u32[]{:S(2)}, u32[]{:S(2)}) collective-permute-start(bf16[272,128]{1,0:T(8,128)(2,1)S(1)} %get-tuple-element.43.t0), channel_id=1, source_target_pairs={{0,56},{8,0},{16,8},{24,16},{32,24},{40,32},{48,40},{56,48},{1,57}... | collective-permute-start | bytes 208904 | tf_op jit(solution)/shard_map/ppermute | solution.py:33
  7.8 6.8 %collective-permute-start.7 = (bf16[272,128]{1,0:T(8,128)(2,1)S(1)}, bf16[272,128]{1,0:T(8,128)(2,1)S(1)}, u32[]{:S(2)}, u32[]{:S(2)}) collective-permute-start(bf16[272,128]{1,0:T(8,128)(2,1)S(1)} %get-tuple-element.43.t0), channel_id=1, source_target_pairs={{0,48},{8,56},{16,0},{24,8},{32,16},{40,24},{48,32},{56,40},{1,49}... | collective-permute-start | bytes 208904 | tf_op jit(solution)/shard_map/ppermute | solution.py:33
  9.3 7.3 %collective-permute-start.8 = (bf16[272,128]{1,0:T(8,128)(2,1)S(1)}, bf16[272,128]{1,0:T(8,128)(2,1)S(1)}, u32[]{:S(2)}, u32[]{:S(2)}) collective-permute-start(bf16[272,128]{1,0:T(8,128)(2,1)S(1)} %get-tuple-element.43.t0), channel_id=1, source_target_pairs={{0,8},{8,16},{16,24},{24,32},{32,40},{40,48},{48,56},{56,0},{1,9},... | collective-permute-start | bytes 208904 | tf_op jit(solution)/shard_map/ppermute | solution.py:33
  10.3 7.5 %collective-permute-start.3 = (s32[2,16,512]{2,1,0:T(8,128)S(1)}, s32[2,16,512]{2,1,0:T(8,128)S(1)}, u32[]{:S(2)}, u32[]{:S(2)}) collective-permute-start(s32[2,16,512]{2,1,0:T(8,128)S(1)} %pad_add_fusion.ids0), channel_id=1, source_target_pairs={{0,128},{64,192},{128,0},{192,64},{1,129},{65,193},{129,1},{193,65... | collective-permute-start | bytes 196616 | tf_op jit(solution)/shard_map/ppermute | solution.py:37
  14.7 14.0 %collective-permute-start.9 = (bf16[544,128]{1,0:T(8,128)(2,1)S(1)}, bf16[544,128]{1,0:T(8,128)(2,1)S(1)}, u32[]{:S(2)}, u32[]{:S(2)}) collective-permute-start(bf16[544,128]{1,0:T(8,128)(2,1)S(1)} %pad_maximum_fusion.1), channel_id=1, source_target_pairs={{0,48},{8,56},{16,0},{24,8},{32,16},{40,24},{48,32},{56,40},{1,49}... | collective-permute-start | bytes 417800 | tf_op jit(solution)/shard_map/ppermute | solution.py:33
  16.6 12.1 %collective-permute-start.10 = (bf16[544,128]{1,0:T(8,128)(2,1)S(1)}, bf16[544,128]{1,0:T(8,128)(2,1)S(1)}, u32[]{:S(2)}, u32[]{:S(2)}) collective-permute-start(bf16[544,128]{1,0:T(8,128)(2,1)S(1)} %pad_maximum_fusion.2), channel_id=1, source_target_pairs={{0,16},{8,24},{16,32},{24,40},{32,48},{40,56},{48,0},{56,8},{1,17}... | collective-permute-start | bytes 417800 | tf_op jit(solution)/shard_map/ppermute | solution.py:33
  30.2 7.1 %collective-permute-start = (bf16[512,128]{1,0:T(8,128)(2,1)S(1)}, bf16[512,128]{1,0:T(8,128)(2,1)S(1)}, u32[]{:S(2)}, u32[]{:S(2)}) collective-permute-start(bf16[512,128]{1,0:T(8,128)(2,1)S(1)} %get-tuple-element.36.fg0), channel_id=1, source_target_pairs={{0,1},{1,0},{2,3},{3,2},{4,5},{5,4},{6,7},{7,6},{8,9},{9,8},{10,11... | collective-permute-start | bytes 393224 | tf_op jit(solution)/shard_map/ppermute | solution.py:37
  33.2 7.9 %collective-permute-start.12 = (bf16[128,512]{1,0:T(8,128)(2,1)S(1)}, bf16[128,512]{1,0:T(8,128)(2,1)S(1)}, u32[]{:S(2)}, u32[]{:S(2)}) collective-permute-start(bf16[128,512]{1,0:T(8,128)(2,1)S(1)} %get-tuple-element.69), channel_id=1, source_target_pairs={{0,128},{64,192},{128,0},{192,64},{1,129},{65,193},{129,1},{193,65... | collective-permute-start | bytes 393224 | tf_op jit(solution)/shard_map/ppermute | solution.py:37
  34.3 7.0 %collective-permute-start.13 = (bf16[128,512]{1,0:T(8,128)(2,1)S(1)}, bf16[128,512]{1,0:T(8,128)(2,1)S(1)}, u32[]{:S(2)}, u32[]{:S(2)}) collective-permute-start(bf16[128,512]{1,0:T(8,128)(2,1)S(1)} %get-tuple-element.71), channel_id=1, source_target_pairs={{0,64},{64,0},{128,192},{192,128},{1,65},{65,1},{129,193},{193,129... | collective-permute-start | bytes 393224 | tf_op jit(solution)/shard_map/ppermute | solution.py:37
  35.0 8.1 %collective-permute-start.14 = (bf16[128,512]{1,0:T(8,128)(2,1)S(1)}, bf16[128,512]{1,0:T(8,128)(2,1)S(1)}, u32[]{:S(2)}, u32[]{:S(2)}) collective-permute-start(bf16[128,512]{1,0:T(8,128)(2,1)S(1)} %get-tuple-element.70), channel_id=1, source_target_pairs={{0,192},{64,128},{128,64},{192,0},{1,193},{65,129},{129,65},{193,1... | collective-permute-start | bytes 393224 | tf_op jit(solution)/shard_map/ppermute | solution.py:37
  37.4 10.0 %collective-permute-start.1 = (bf16[1024,128]{1,0:T(8,128)(2,1)S(1)}, bf16[1024,128]{1,0:T(8,128)(2,1)S(1)}, u32[]{:S(2)}, u32[]{:S(2)}) collective-permute-start(bf16[1024,128]{1,0:T(8,128)(2,1)S(1)} %pad_maximum_fusion), channel_id=1, source_target_pairs={{0,2},{1,3},{2,0},{3,1},{4,6},{5,7},{6,4},{7,5},{8,10},{9,11},{10,... | collective-permute-start | bytes 786440 | tf_op jit(solution)/shard_map/ppermute | solution.py:37
  43.2 8.0 %collective-permute-start.15 = (bf16[128,512]{1,0:T(8,128)(2,1)S(1)}, bf16[128,512]{1,0:T(8,128)(2,1)S(1)}, u32[]{:S(2)}, u32[]{:S(2)}) collective-permute-start(bf16[128,512]{1,0:T(8,128)(2,1)S(1)} %fusion.3.s0), channel_id=1, source_target_pairs={{0,2},{1,3},{2,0},{3,1},{4,6},{5,7},{6,4},{7,5},{8,10},{9,11},{10,... | collective-permute-start | bytes 393224 | tf_op jit(solution)/shard_map/ppermute | solution.py:37
  44.6 7.3 %collective-permute-start.16 = (bf16[128,512]{1,0:T(8,128)(2,1)S(1)}, bf16[128,512]{1,0:T(8,128)(2,1)S(1)}, u32[]{:S(2)}, u32[]{:S(2)}) collective-permute-start(bf16[128,512]{1,0:T(8,128)(2,1)S(1)} %fusion.3.s0), channel_id=1, source_target_pairs={{0,1},{1,0},{2,3},{3,2},{4,5},{5,4},{6,7},{7,6},{8,9},{9,8},{10,11... | collective-permute-start | bytes 393224 | tf_op jit(solution)/shard_map/ppermute | solution.py:37
  45.7 7.3 %collective-permute-start.17 = (bf16[128,512]{1,0:T(8,128)(2,1)S(1)}, bf16[128,512]{1,0:T(8,128)(2,1)S(1)}, u32[]{:S(2)}, u32[]{:S(2)}) collective-permute-start(bf16[128,512]{1,0:T(8,128)(2,1)S(1)} %fusion.3.s0), channel_id=1, source_target_pairs={{0,3},{1,2},{2,1},{3,0},{4,7},{5,6},{6,5},{7,4},{8,11},{9,10},{10,... | collective-permute-start | bytes 393224 | tf_op jit(solution)/shard_map/ppermute | solution.py:37
  54.8 9.3 %collective-permute-start.18 = (bf16[768,128]{1,0:T(8,128)(2,1)S(1)}, bf16[768,128]{1,0:T(8,128)(2,1)S(1)}, u32[]{:S(2)}, u32[]{:S(2)}) collective-permute-start(bf16[768,128]{1,0:T(8,128)(2,1)S(1)} %get-tuple-element.48.m0), channel_id=1, source_target_pairs={{0,128},{64,192},{128,0},{192,64},{1,129},{65,193},{129,1},{193,65... | collective-permute-start | bytes 589832 | tf_op jit(solution)/shard_map/ppermute | solution.py:37
  55.7 8.7 %collective-permute-start.19 = (bf16[768,128]{1,0:T(8,128)(2,1)S(1)}, bf16[768,128]{1,0:T(8,128)(2,1)S(1)}, u32[]{:S(2)}, u32[]{:S(2)}) collective-permute-start(bf16[768,128]{1,0:T(8,128)(2,1)S(1)} %get-tuple-element.48.m0), channel_id=1, source_target_pairs={{0,64},{64,0},{128,192},{192,128},{1,65},{65,1},{129,193},{193,129... | collective-permute-start | bytes 589832 | tf_op jit(solution)/shard_map/ppermute | solution.py:37
  56.0 11.3 %collective-permute-start.20 = (bf16[768,128]{1,0:T(8,128)(2,1)S(1)}, bf16[768,128]{1,0:T(8,128)(2,1)S(1)}, u32[]{:S(2)}, u32[]{:S(2)}) collective-permute-start(bf16[768,128]{1,0:T(8,128)(2,1)S(1)} %get-tuple-element.48.m0), channel_id=1, source_target_pairs={{0,192},{64,128},{128,64},{192,0},{1,193},{65,129},{129,65},{193,1... | collective-permute-start | bytes 589832 | tf_op jit(solution)/shard_map/ppermute | solution.py:37
  58.9 9.4 %collective-permute-start.21 = (bf16[768,128]{1,0:T(8,128)(2,1)S(1)}, bf16[768,128]{1,0:T(8,128)(2,1)S(1)}, u32[]{:S(2)}, u32[]{:S(2)}) collective-permute-start(bf16[768,128]{1,0:T(8,128)(2,1)S(1)} %get-tuple-element.48.m0), channel_id=1, source_target_pairs={{0,4},{4,0},{1,5},{5,1},{2,6},{6,2},{3,7},{7,3},{8,12},{12,8},{9,1... | collective-permute-start | bytes 589832 | tf_op jit(solution)/shard_map/ppermute | solution.py:37
  69.9 7.4 %collective-permute-start.25 = (bf16[528,128]{1,0:T(8,128)(2,1)S(1)}, bf16[528,128]{1,0:T(8,128)(2,1)S(1)}, u32[]{:S(2)}, u32[]{:S(2)}) collective-permute-start(bf16[528,128]{1,0:T(8,128)(2,1)S(1)} %get-tuple-element.49.first), channel_id=1, source_target_pairs={{0,8},{8,16},{16,24},{24,32},{32,40},{40,48},{48,56},{56,0},{1,9},... | collective-permute-start | bytes 405512 | tf_op jit(solution)/shard_map/ppermute | solution.py:33
  70.3 7.0 %collective-permute-start.26 = (f32[16,128]{1,0:T(8,128)S(1)}, f32[16,128]{1,0:T(8,128)S(1)}, u32[]{:S(2)}, u32[]{:S(2)}) collective-permute-start(f32[16,128]{1,0:T(8,128)S(1)} %get-tuple-element.51), channel_id=1, source_target_pairs={{0,16},{8,24},{16,32},{24,40},{32,48},{40,56},{48,0},{56,8},{1,17}... | collective-permute-start | bytes 24584 | tf_op jit(solution)/shard_map/ppermute | solution.py:33
  71.4 7.2 %collective-permute-start.28 = (bf16[528,128]{1,0:T(8,128)(2,1)S(1)}, bf16[528,128]{1,0:T(8,128)(2,1)S(1)}, u32[]{:S(2)}, u32[]{:S(2)}) collective-permute-start(bf16[528,128]{1,0:T(8,128)(2,1)S(1)} %get-tuple-element.53), channel_id=1, source_target_pairs={{0,56},{8,0},{16,8},{24,16},{32,24},{40,32},{48,40},{56,48},{1,57}... | collective-permute-start | bytes 405512 | tf_op jit(solution)/shard_map/ppermute | solution.py:33
  77.3 6.3 %collective-permute-start.27 = (bf16[528,128]{1,0:T(8,128)(2,1)S(1)}, bf16[528,128]{1,0:T(8,128)(2,1)S(1)}, u32[]{:S(2)}, u32[]{:S(2)}) collective-permute-start(bf16[528,128]{1,0:T(8,128)(2,1)S(1)} %get-tuple-element.52), channel_id=1, source_target_pairs={{0,8},{8,16},{16,24},{24,32},{32,40},{40,48},{48,56},{56,0},{1,9},... | collective-permute-start | bytes 405512 | tf_op jit(solution)/shard_map/ppermute | solution.py:33
  83.6 6.3 %collective-permute-start.29 = (bf16[528,128]{1,0:T(8,128)(2,1)S(1)}, bf16[528,128]{1,0:T(8,128)(2,1)S(1)}, u32[]{:S(2)}, u32[]{:S(2)}) collective-permute-start(bf16[528,128]{1,0:T(8,128)(2,1)S(1)} %get-tuple-element.56), channel_id=1, source_target_pairs={{0,8},{8,16},{16,24},{24,32},{32,40},{40,48},{48,56},{56,0},{1,9},... | collective-permute-start | bytes 405512 | tf_op jit(solution)/shard_map/ppermute | solution.py:33
  (12 other events, 88.4 us)
